TPU v7x, 256 devices: a whole 4x4x8 slice. The times are simulated.
256 devices in a mesh: head: 16 (over z, x_hi), ctx: 16 (over y, x_lo, core).
Axes of the slice: x: 4 (x_hi: 2, x_lo: 2; x = x_hi * 2 + x_lo), y: 4, z: 8, core: 2. Of those that a mesh axis runs over, the one named last changes fastest.
Arguments:
- queries: bfloat16 [32768, 2048], P(('head', 'ctx')), may hold values from -16 to 16
- keys: bfloat16 [32768, 256], P(('head', 'ctx')), may hold values from -16 to 16
- values: bfloat16 [32768, 256], P(('head', 'ctx')), may hold values from -6 to 6
- lengths: int32 [16], replicated, may hold values from 1 to 384, 512 in all
Outputs:
- attended: bfloat16 [32768, 2048], P(('head', 'ctx'))
All inputs are finite; a program needn't handle non-finite values.
Results may differ from a plain program's by a relative error of at most 0.006.
Values may be sent and summed in bfloat16 or wider, within the bound.
No kernel may reach another device: no remote copies, remote signals or barrier semaphores. Data moves between devices by JAX's collectives and lax.ppermute only.
A program may use at most 64 MiB of HBM per device.

v0:
```python
import math

import jax
import jax.numpy as jnp
from jax import lax
from jax.sharding import PartitionSpec as P

HD = 128
BLOCK = 64


def doc_lookup(where_at, doc_ends):
    return jnp.sum((where_at[:, None] >= doc_ends[None, :]).astype(jnp.int32), axis=1)


def shards(queries, keys, values, lengths):
    n_heads = lax.axis_size("head")
    n_context = lax.axis_size("ctx")
    ctx_index = lax.axis_index("ctx")
    head_index = lax.axis_index("head")
    segment = queries.shape[0]
    kv_count = keys.shape[1] // HD
    per_device = queries.shape[1] // HD // n_heads
    repeat = n_heads // kv_count
    kv_select = head_index // repeat
    doc_ends = jnp.cumsum(lengths) * BLOCK
    scale = 1.0 / HD**0.5
    local_queries = lax.all_to_all(queries, "head", split_axis=1, concat_axis=0, tiled=True)
    rows = local_queries.shape[0]
    row_ids = jnp.arange(rows, dtype=jnp.int32)
    query_pos = row_ids // segment * (segment * n_context) + ctx_index * segment + row_ids % segment
    query_doc = doc_lookup(query_pos, doc_ends)
    query_mat = local_queries.reshape(rows, per_device, HD)
    initial = (
        jnp.full((rows, per_device), -1e30, jnp.float32),
        jnp.zeros((rows, per_device), jnp.float32),
        jnp.zeros((rows, per_device, HD), jnp.float32),
    )
    keys_group, values_group = (
        lax.all_gather(keys, "head", axis=0, tiled=True),
        lax.all_gather(values, "head", axis=0, tiled=True),
    )
    keys_local = lax.dynamic_slice_in_dim(keys_group, kv_select * HD, HD, 1)
    values_local = lax.dynamic_slice_in_dim(values_group, kv_select * HD, HD, 1)
    shard_rows = keys_local.shape[0]
    pieces = (
        lax.all_gather(keys_local, "ctx", axis=0, tiled=True),
        lax.all_gather(values_local, "ctx", axis=0, tiled=True),
    )
    count = pieces[0].shape[0]
    flat = jnp.arange(count, dtype=jnp.int32)
    owner = flat // shard_rows
    inside = flat % shard_rows
    key_pos = inside // segment * (segment * n_context) + owner * segment + inside % segment
    key_rows = pieces[0]
    value_rows = pieces[1]
    count = key_rows.shape[0]
    width = math.gcd(count, 512)

    def step(index, state):
        first = index * width
        key_block = lax.dynamic_slice_in_dim(key_rows, first, width, 0)
        value_block = lax.dynamic_slice_in_dim(value_rows, first, width, 0)
        block_pos = lax.dynamic_slice_in_dim(key_pos, first, width, 0)
        block_doc = doc_lookup(block_pos, doc_ends)
        allowed = (query_doc[:, None] == block_doc[None, :]) & (
            block_pos[None, :] <= query_pos[:, None]
        )

        def live(inner):
            running, total, accum = inner
            scores = (
                jnp.einsum("rhd,kd->rhk", query_mat, key_block, preferred_element_type=jnp.float32)
                * scale
            )
            scores = jnp.where(allowed[:, None, :], scores, -jnp.inf)
            newest = jnp.maximum(running, jnp.max(scores, axis=2))
            factor = jnp.exp(running - newest)
            expo = jnp.exp(scores - newest[:, :, None])
            total = total * factor + jnp.sum(expo, axis=2)
            weights = expo.astype(jnp.bfloat16)
            accum = accum * factor[:, :, None] + jnp.einsum(
                "rhk,kd->rhd", weights, value_block, preferred_element_type=jnp.float32
            )
            return (newest, total, accum)

        return lax.cond(jnp.any(allowed), live, lambda inner: inner, state)

    final = lax.fori_loop(0, count // width, step, initial)
    running, total, accum = final
    output = (accum / total[:, :, None]).astype(jnp.bfloat16).reshape(rows, per_device * HD)
    return lax.all_to_all(output, "head", split_axis=0, concat_axis=1, tiled=True)


def solution(mesh):
    return jax.shard_map(
        shards,
        mesh=mesh,
        in_specs=(
            P(("head", "ctx"), None),
            P(("head", "ctx"), None),
            P(("head", "ctx"), None),
            P(),
        ),
        out_specs=P(("head", "ctx"), None),
        check_vma=False,
    )
```

profile of v0, /device:TPU:6, one launch (start us, length us, event | category | flops | bytes accessed | tf_op | source)
XLA Modules:
  0.0 808.1 jit_solution(18104520876869166776)
XLA Ops:
  8.1 82.1 %all-gather.5.cloned.1.call-done = bf16[2048,256]{1,0:T(8,128)(2,1)} async-done(((bf16[128,256]{1,0:T(8,128)(2,1)}), bf16[2048,256]{1,0:T(8,128)(2,1)}) %all-gather.5.cloned.1.call-update) | async-done | bytes 1048592 | tf_op jit(solution)/shard_map/all_gather | solution.py:40
  92.1 76.1 %all-gather.9.cloned.1.call-done = bf16[2048,256]{1,0:T(8,128)(2,1)} async-done(((bf16[128,256]{1,0:T(8,128)(2,1)}), bf16[2048,256]{1,0:T(8,128)(2,1)}) %all-gather.9.cloned.1.call-update) | async-done | bytes 1048592 | tf_op jit(solution)/shard_map/all_gather | solution.py:41
  172.1 7.1 all-to-all-start
  179.6 12.4 %all-to-all-done = bf16[128,16,128]{0,2,1:T(8,128)(2,1)S(1)} async-done(((bf16[128,16,128]{0,2,1:T(8,128)(2,1)}), bf16[128,16,128]{0,2,1:T(8,128)(2,1)S(1)}, u32[]{:S(2)}, u32[]{:S(2)}) %all-to-all-start) | async-done | bytes 524320 | tf_op jit(solution)/shard_map/all_to_all | solution.py:28
  192.3 34.5 %all-gather.7.cloned.1.call-done = bf16[32768,128]{1,0:T(8,128)(2,1)} async-done(((bf16[2048,128]{1,0:T(8,128)(2,1)}), bf16[32768,128]{1,0:T(8,128)(2,1)}) %all-gather.7.cloned.1.call-update) | async-done | bytes 8388624 | tf_op jit(solution)/shard_map/all_gather | solution.py:47
  226.8 57.1 %all-gather.11.cloned.1.call-done = bf16[32768,128]{1,0:T(8,128)(2,1)} async-done(((bf16[2048,128]{1,0:T(8,128)(2,1)}), bf16[32768,128]{1,0:T(8,128)(2,1)}) %all-gather.11.cloned.1.call-update) | async-done | bytes 8388624 | tf_op jit(solution)/shard_map/all_gather | solution.py:48
  284.0 489.4 %while.18 = (s32[]{:T(128)}, f32[2048,1]{0,1:T(1,128)S(1)}, f32[2048,1]{0,1:T(1,128)S(1)}, f32[2048,1,128]{2,0,1:T(8,128)S(1)}, s32[2048]{0:T(1024)S(1)}, /*inde...) while((s32[]{:T(128)}, f32[2048,1]{0,1:T(1,128)S(1)}, ...), condition=%wide.region_9.10_spmd.clone, body=%wide.region_2.9_spmd.clone.sunk | while | flops 548988416 | bytes 17732992 | solution.py:89
  286.7 4.9 conditional.3
  294.4 4.9 conditional.3
  309.7 4.9 conditional.3
  317.3 4.9 conditional.3
  325.0 4.9 conditional.3
  332.6 4.9 conditional.3
  347.9 4.9 conditional.3
  355.6 4.9 conditional.3
  363.2 4.9 conditional.3
  378.5 4.9 conditional.3
  386.1 4.9 conditional.3
  393.8 4.9 conditional.3
  401.4 4.9 conditional.3
  416.7 4.9 conditional.3
  424.4 4.9 conditional.3
  432.0 4.9 conditional.3
  439.7 4.9 conditional.3
  455.0 4.9 conditional.3
  462.6 4.9 conditional.3
  470.3 4.9 conditional.3
  477.9 4.9 conditional.3
  493.2 4.9 conditional.3
  500.8 4.9 conditional.3
  508.5 4.9 conditional.3
  773.7 26.6 %all_to_all.35 = bf16[16,128,128]{2,1,0:T(8,128)(2,1)S(1)} all-to-all(bf16[16,128,128]{2,1,0:T(8,128)(2,1)S(1)} %bitcast.27), channel_id=1, replica_groups=mesh['head'=16,'ctx'=16] {'head'}, dimensions={0} | all-to-all | bytes 1048576 | tf_op jit(solution)/shard_map/all_to_all | solution.py:92
  (706 shorter events, 648.9 us)
Async XLA Ops:
  6.5 172.6 %copy-start = (s32[16]{0:T(128)S(1)}, s32[16]{0:T(128)}, u32[]{:S(2)}) copy-start(s32[16]{0:T(128)} %param.11) | copy-start | bytes 196
  6.5 83.6 %all-gather.5.cloned.1.call-start = ((), (), s32[]{:S(2)}) async-start(), calls=%async_computation.2 | async-start | bytes 1114112 | tf_op jit(solution)/shard_map/all_gather | solution.py:40
  7.3 160.9 %all-gather.9.cloned.1.call-start = ((), (), s32[]{:S(2)}) async-start(), calls=%async_computation.4 | async-start | bytes 1114112 | tf_op jit(solution)/shard_map/all_gather | solution.py:41
  8.0 218.8 %all-gather.7.cloned.1.call-start = ((), (), s32[]{:S(2)}) async-start(), calls=%async_computation.3 | async-start | bytes 8912896 | tf_op jit(solution)/shard_map/all_gather | solution.py:47
  92.1 191.8 %all-gather.11.cloned.1.call-start = ((), (), s32[]{:S(2)}) async-start(), calls=%async_computation.5 | async-start | bytes 8912896 | tf_op jit(solution)/shard_map/all_gather | solution.py:48
  172.1 19.9 %all-to-all-start = ((bf16[128,16,128]{0,2,1:T(8,128)(2,1)}), bf16[128,16,128]{0,2,1:T(8,128)(2,1)S(1)}, u32[]{:S(2)}, u32[]{:S(2)}) async-start(bf16[128,16,128]{0,2,1:T(8,128)(2,1)} %bitcast.8), calls=%async_computation | async-start | bytes 1048576 | tf_op jit(solution)/shard_map/all_to_all | solution.py:28
Sparse Core Ops, SparseCore 0:
  9.9 80.1 all-gather.4
  92.8 75.3 all-gather.8
  170.0 56.6 all-gather.6
  228.5 55.3 all-gather.10
where the time goes:
time: 818 us; the launch traced here: 808 us
  waiting for transfers between devices  264 us (32%)
  matrix products  264 us (32%)
  other arithmetic  177 us (22%)
  loops' own time  44.5 us (5%)
  blocking collectives  26.6 us (3%)
  between operations  13.2 us (2%)
  local copies, waits for them, and re-layouts  12.6 us (2%)
    dot_general x64, matrix products, live(): jnp.einsum('rhk,kd->rhd', weights, value_block, preferred_element_type=jn...  150 us
    reduce_or x64, other arithmetic, step(): return lax.cond(jnp.any(allowed), live, lambda inner: inner, state)  126 us
    dot_general x64, matrix products, live(): jnp.einsum('rhd,kd->rhk', query_mat, key_block, preferred_element_type=jn...  114 us
    all_gather x1, waiting for transfers between devices, shards(): lax.all_gather(keys, 'head', axis=0, tiled=True)  82.1 us
    all_gather x1, waiting for transfers between devices, shards(): lax.all_gather(values, 'head', axis=0, tiled=True)  76.1 us
    all_gather x1, waiting for transfers between devices, shards(): lax.all_gather(values_local, 'ctx', axis=0, tiled=True)  57.1 us
    another operation x1, loops' own time, shards(): final = lax.fori_loop(0, count // width, step, initial)  41.5 us
    reduce_sum x64, other arithmetic, live(): total = total * factor + jnp.sum(expo, axis=2)  41.1 us
  transfers between devices with their start and end apart: 5, of which 5 were waited for; matrix products, arithmetic and copies ran while one was open for 1% of the time, Pallas kernels for 0%

commit v1 on v0

v1 whole, which is shorter than its diff:
```python
import functools
import math

import jax
import jax.numpy as jnp
from jax import lax
from jax.experimental import pallas as pl
from jax.experimental.pallas import tpu as pltpu
from jax.sharding import Mesh, PartitionSpec as P

HD = 128
BLOCK = 64
AXES = ("z", "xh", "y", "xl", "c")
SIZES = (8, 2, 4, 2, 2)
PLANE = 4096
TILE = 128
MASKED = -2e30
FLOOR = -1e29
LOG2E_SCALE = math.log2(math.e) / math.sqrt(HD)
RC = 8
WIDE = RC * TILE
SPAN = 2 * WIDE
PER = PLANE // SPAN


def attend_kernel(info, q_own, q_other, kv, o_own, o_other, lse_own, lse_other,
                  qq, acc, peak, total, score, weight, top, fade, units):
    place = info[0]
    core = info[1]
    for half, ref in enumerate((q_own, q_other)):
        for head in range(2):
            full = ref[:, head].astype(jnp.float32) * LOG2E_SCALE
            high = full.astype(jnp.bfloat16)
            lanes = slice(head * 256 + half * 128, head * 256 + half * 128 + 128)
            qq[:, :HD, lanes] = high
            qq[:, HD:, lanes] = (full - high.astype(jnp.float32)).astype(jnp.bfloat16)
    acc[...] = jnp.zeros_like(acc)
    total[...] = jnp.zeros_like(total)
    peak[...] = jnp.full_like(peak, FLOOR)

    def keys_of(n):
        return kv[pl.ds((n % PER) * RC, RC), n // PER]

    def bounds(z):
        lane = lax.broadcasted_iota(jnp.int32, (1, 512), 1) % 256
        b = lane // 64
        at = 4 + z * 6
        start = jnp.where(b == 0, info[at], jnp.where(b == 1, info[at + 1],
                          jnp.where(b == 2, info[at + 2], info[at + 3])))
        part = jnp.where(lane < 128, core, 1 - core) * 128
        return start, z * PLANE + place + part + lane % 128

    def scores_of(z, n, masked):
        k = keys_of(n)[:, :, :HD].reshape(WIDE, HD)
        s = jnp.dot(jnp.concatenate([k, k], axis=1), qq[z], preferred_element_type=jnp.float32)
        if masked:
            start, stop = bounds(z)
            row = lax.broadcasted_iota(jnp.int32, (TILE, 512), 0)
            parts = []
            for g in range(RC):
                base = n * SPAN + g * 256 + core * TILE
                keep = (row >= start - base) & (row <= stop - base)
                parts.append(jnp.where(keep, s[g * TILE:(g + 1) * TILE], MASKED))
            s = jnp.concatenate(parts, axis=0)
        score[...] = s
        top[...] = jnp.max(s.reshape(WIDE // 8, 8, 512), axis=0)

    def weigh(z):
        old = peak[z]
        new = jnp.maximum(old, jnp.max(top[...], axis=0, keepdims=True))
        factor = jnp.exp2(old - new)
        fade[...] = factor
        peak[z] = new
        sums = total[z] * factor
        for u in range(WIDE // 16):
            rows = slice(u * 16, u * 16 + 16)
            p = jnp.exp2(score[rows, :].reshape(2, 8, 512) - new)
            sums = sums + (p[0] + p[1])
            weight[rows, :] = p.reshape(16, 512).astype(jnp.bfloat16)
        total[z] = sums

    def gather(z, n):
        v = keys_of(n)[:, :, HD:]
        pv = jnp.dot(jnp.concatenate([v[g] for g in range(RC)], axis=1), weight[...],
                     preferred_element_type=jnp.float32)
        acc[z] = (acc[z].reshape(16, 8, 512) * fade[...] + pv.reshape(16, 8, 512)).reshape(HD, 512)

    def run(masked):
        def build(z, count):
            first = info[4 + z * 6 + 4] // SPAN
            last = (z * PLANE + place) // SPAN
            clear = jnp.minimum((info[4 + z * 6 + 5] + SPAN - 1) // SPAN, last)

            def put(n, count):
                units[count] = z * 256 + n
                return count + 1

            if masked:
                return lax.fori_loop(first, clear, put, put(last, count))
            return lax.fori_loop(clear, last, put, count)

        count = lax.fori_loop(0, 8, build, 0)

        def at(i):
            return units[i] // 256, units[i] % 256

        @pl.when(count > 0)
        def _():
            scores_of(*at(0), masked)
            weight[...] = jnp.zeros_like(weight)
            fade[...] = jnp.ones_like(fade)

            def body(i, carry):
                z, n = at(i)
                gather(*at(jnp.maximum(i - 1, 0)))
                weigh(z)
                scores_of(*at(jnp.minimum(i + 1, count - 1)), masked)
                return carry

            lax.fori_loop(0, count, body, 0)
            gather(*at(count - 1))

    run(True)
    run(False)
    for z in range(8):
        l = jnp.sum(total[z], axis=0, keepdims=True)
        o = acc[z] / jnp.where(l > 0, l, 1.0)
        lse = jnp.where(l > 0, peak[z, :1] + jnp.log2(jnp.where(l > 0, l, 1.0)), FLOOR)
        for head in range(2):
            for half, (o_ref, lse_ref) in enumerate(((o_own, lse_own), (o_other, lse_other))):
                lanes = slice(head * 256 + half * 128, head * 256 + half * 128 + 128)
                o_ref[z, head] = o[:, lanes].astype(o_ref.dtype)
                lse_ref[z, head] = jnp.broadcast_to(lse[:, lanes], (8, TILE))


def attend(info, q_own, q_other, kv):
    vmem = pltpu.VMEM
    f32, bf16 = jnp.float32, jnp.bfloat16
    o = jax.ShapeDtypeStruct((8, 2, HD, TILE), bf16)
    lse = jax.ShapeDtypeStruct((8, 2, 8, TILE), f32)
    return pl.pallas_call(
        attend_kernel,
        out_shape=(o, o, lse, lse),
        in_specs=[pl.BlockSpec(memory_space=pltpu.SMEM)] + [pl.BlockSpec(memory_space=vmem)] * 3,
        out_specs=[pl.BlockSpec(memory_space=vmem)] * 4,
        scratch_shapes=[
            vmem((8, 2 * HD, 512), bf16),
            vmem((8, HD, 512), f32),
            vmem((8, 8, 512), f32),
            vmem((8, 8, 512), f32),
            vmem((WIDE, 512), f32),
            vmem((WIDE, 512), bf16),
            vmem((8, 512), f32),
            vmem((8, 512), f32),
            pltpu.SMEM((8 * PER * 8 + 16,), jnp.int32),
        ],
        compiler_params=pltpu.CompilerParams(vmem_limit_bytes=48 * 2**20),
    )(info, q_own, q_other, kv)


def positions(lengths):
    core = lax.axis_index("c")
    place = (lax.axis_index("xh") * 8 + lax.axis_index("y") * 2 + lax.axis_index("xl")) * 256
    ends = jnp.cumsum(lengths) * BLOCK
    b = jnp.arange(4, dtype=jnp.int32)
    own_first = jnp.where(b < 2, core, 1 - core) * 128 + (b % 2) * 64
    offsets = jnp.concatenate([own_first, jnp.array([0, 192], jnp.int32)])
    tokens = jnp.arange(8, dtype=jnp.int32)[:, None] * PLANE + place + offsets[None, :]
    starts = jnp.max(jnp.where(ends[None, None, :] <= tokens[:, :, None], ends[None, None, :], 0), axis=2)
    head = jnp.stack([place, core, core, core])
    return jnp.concatenate([head, starts.reshape(48)]).astype(jnp.int32)


def shards(queries, keys, values, lengths):
    swap = [(0, 1), (1, 0)]
    k = keys.reshape(TILE, 2, HD).transpose(1, 0, 2)
    vt = values.reshape(TILE, 2, HD).transpose(1, 2, 0)
    kv = jnp.concatenate([k, vt], axis=2)
    kv_send = jnp.repeat(kv, 4, axis=0)
    kv_z = lax.all_to_all(kv_send, "z", split_axis=0, concat_axis=0, tiled=True)
    kv_all = lax.all_gather(kv_z, ("xh", "y", "xl"), axis=0, tiled=False)
    qt = queries.reshape(TILE, 8, 2, HD).transpose(1, 2, 3, 0)
    q_own = lax.all_to_all(qt, "z", split_axis=0, concat_axis=0, tiled=True)
    q_other = lax.ppermute(q_own, "c", swap)
    info = positions(lengths)
    o_own, o_other, lse_own, lse_other = attend(info, q_own, q_other, kv_all.reshape(16, 8, TILE, 2 * HD))
    o_got = lax.ppermute(o_other, "c", swap)
    lse_got = lax.ppermute(lse_other, "c", swap)
    a, b = lse_own[:, :, :1], lse_got[:, :, :1]
    most = jnp.maximum(a, b)
    wa, wb = jnp.exp2(a - most), jnp.exp2(b - most)
    o = (o_own.astype(jnp.float32) * wa + o_got.astype(jnp.float32) * wb) / (wa + wb)
    back = lax.all_to_all(o.astype(jnp.bfloat16), "z", split_axis=0, concat_axis=0, tiled=True)
    return back.transpose(3, 0, 1, 2).reshape(TILE, 16 * HD)


def solution(mesh):
    fine = Mesh(mesh.devices.reshape(SIZES), AXES)
    spec = P(AXES, None)
    return jax.shard_map(
        shards, mesh=fine, in_specs=(spec, spec, spec, P()), out_specs=spec, check_vma=False
    )
```

time: 818 us -> 289 us (0.35); the launches traced: 808 us -> 289 us
  matrix products: 264 us -> 0 us
  other arithmetic: 177 us -> 1.03 us
  waiting for transfers between devices: 264 us -> 174 us
  loops' own time: 44.5 us -> 0 us
  Pallas kernels: 0 us -> 40 us
  blocking collectives: 26.6 us -> 50.5 us
    dot_general x128 -> x0, matrix products: 264 us -> none  [the longest x64 150 us: live(): jnp.einsum('rhk,kd->rhd', weights, value_block, preferred_element_type=jn...]
    reduce_or x64 -> x0, other arithmetic: 126 us -> none  [step(): return lax.cond(jnp.any(allowed), live, lambda inner: inner, state)]
    all_gather x4 -> x1, waiting for transfers between devices: 250 us -> 156 us  [shards(): kv_all = lax.all_gather(kv_z, ('xh', 'y', 'xl'), axis=0, tiled=False)]
    reduce_sum x129 -> x0, other arithmetic: 47 us -> none  [the longest x64 41.1 us: live(): total = total * factor + jnp.sum(expo, axis=2)]
    another operation x65 -> x0, loops' own time: 44.5 us -> none  [the longest x1 41.5 us: shards(): final = lax.fori_loop(0, count // width, step, initial)]
    pallas_call x0 -> x1, Pallas kernels: none -> 40 us  [attend(): pl.pallas_call(attend_kernel, out_shape=(o, o, lse, lse), in_specs=[pl.Bl...]
    all_to_all x1 -> x2, blocking collectives: 26.6 us -> 50.5 us  [the longest x1 25.9 us: shards(): kv_z = lax.all_to_all(kv_send, 'z', split_axis=0, concat_axis=0, tiled=True)]
    dynamic_slice x66 -> x0, local copies, waits for them, and re-layouts: 8.68 us -> none  [the longest x64 4.95 us: step(): block_pos = lax.dynamic_slice_in_dim(key_pos, first, width, 0)]
  transfers between devices with their start and end apart: 5 -> 5, of which waited for: 5 -> 4; matrix products, arithmetic and copies ran while one was open for 1% -> 1% of each run, Pallas kernels for 0% -> 0%
where the time goes in v1:
time: 289 us
  waiting for transfers between devices  174 us (60%)
  blocking collectives  50.5 us (17%)
  Pallas kernels  40 us (14%)
  between operations  13.5 us (5%)
  local copies, waits for them, and re-layouts  6.03 us (2%)
  starting transfers between devices  4.09 us (1%)
    all_gather x1, waiting for transfers between devices, shards(): kv_all = lax.all_gather(kv_z, ('xh', 'y', 'xl'), axis=0, tiled=False)  156 us
    pallas_call x1, Pallas kernels, attend(): pl.pallas_call(attend_kernel, out_shape=(o, o, lse, lse), in_specs=[pl.Bl...  40 us
    all_to_all x1, blocking collectives, shards(): kv_z = lax.all_to_all(kv_send, 'z', split_axis=0, concat_axis=0, tiled=True)  25.9 us
    all_to_all x1, blocking collectives, shards(): lax.all_to_all(o.astype(jnp.bfloat16), 'z', split_axis=0, concat_axis=0,...  24.6 us
    all_to_all x1, waiting for transfers between devices, shards(): q_own = lax.all_to_all(qt, 'z', split_axis=0, concat_axis=0, tiled=True)  15.1 us
  transfers between devices with their start and end apart: 5, of which 4 were waited for; matrix products, arithmetic and copies ran while one was open for 1% of the time, Pallas kernels for 0%

profile of v1, /device:TPU:6, one launch (start us, length us, event | category | flops | bytes accessed | tf_op | source)
XLA Modules:
  0.0 288.7 jit_solution(7936167473278356790)
XLA Ops:
  6.5 0.0 all-gather.3.cloned.1.call-start
  6.5 0.9 reshape.81
  7.4 0.1 copy.24
  7.5 0.9 reshape.82
  8.4 0.2 pad_maximum_fusion
  8.6 0.1 copy.25
  8.7 25.9 %all_to_all.15 = bf16[8,128,256]{2,1,0:T(8,128)(2,1)} all-to-all(bf16[8,128,256]{2,1,0:T(8,128)(2,1)S(1)} %bitcast.17), channel_id=1, replica_groups=mesh['z'=8,'xh'=2,'y'=4,'xl'=2,'c'=2] {'z'}, dimensions={0} | all-to-all | bytes 1048576 | tf_op jit(solution)/shard_map/all_to_all | solution.py:180
  34.6 0.0 all-gather.3.cloned.1.call-update
  34.6 2.0 copy.23
  36.7 3.5 %all-to-all-start = ((bf16[8,2,128,128]{3,2,1,0:T(8,128)(2,1)}), bf16[8,2,128,128]{3,2,1,0:T(8,128)(2,1)S(1)}, u32[]{:S(2)}, u32[]{:S(2)}) async-start(bf16[8,2,128,128]{3,2,1,0:T(8,128)(2,1)} %bitcast.4), calls=%async_computation | async-start | bytes 1048576 | tf_op jit(solution)/shard_map/all_to_all | solution.py:183
  40.2 0.7 copy.21
  41.0 15.1 %all-to-all-done.q_own = bf16[8,2,128,128]{3,2,1,0:T(8,128)(2,1)S(1)} async-done(((bf16[8,2,128,128]{3,2,1,0:T(8,128)(2,1)}), bf16[8,2,128,128]{3,2,1,0:T(8,128)(2,1)S(1)}, u32[]{:S(2)}, u32[]{:S(2)}) %all-to-all-start) | async-done | bytes 524320 | tf_op jit(solution)/shard_map/all_to_all | solution.py:183
  56.1 0.0 collective-permute-start
  56.1 0.1 pad_add_fusion
  56.2 0.1 multiply_reduce_fusion
  56.3 0.1 broadcast_add_fusion
  56.3 0.3 select_reduce_fusion
  56.6 0.1 copy.22
  56.7 0.1 reshape.79
  56.8 0.1 concatenate.10.info
  56.8 1.1 collective-permute-done.q_other
  58.0 155.8 %all-gather.3.cloned.1.call-done = bf16[128,128,256]{2,1,0:T(8,128)(2,1)} async-done(((bf16[8,128,256]{2,1,0:T(8,128)(2,1)}), bf16[128,128,256]{2,1,0:T(8,128)(2,1)}) %all-gather.3.cloned.1.call-update) | async-done | bytes 8388624 | tf_op jit(solution)/shard_map/all_gather | solution.py:181
  213.8 40.0 %shard_map.55 = (bf16[8,2,128,128]{3,2,1,0:T(8,128)(2,1)S(1)}, bf16[8,2,128,128]{3,2,1,0:T(8,128)(2,1)S(1)}, f32[8,2,8,128]{3,2,1,0:T(8,128)S(1)}, f32[8,2,8,128]{3,2,1,0:T(8,128)S(1)}) custom-call(s32[52]{0:T(128)S(1)} %concatenate.10.info, bf16[8,2,128,128]{3,2,1,0:T(8,128)(2,1)S(1)} %all-to-all-done.q_own, ...), custom_call_target="tpu_custom_call" | custom-call | tf_op jit(solution)/shard_map/pallas_call | solution.py:141
  253.8 0.1 collective-permute-start.2
  253.9 0.5 collective-permute-start.1
  254.4 1.5 collective-permute-done.1
  255.9 0.0 collective-permute-done.2
  255.9 0.3 divide_convert_fusion
  256.2 24.6 %all_to_all.16 = bf16[8,2,128,128]{3,2,1,0:T(8,128)(2,1)S(1)} all-to-all(bf16[8,2,128,128]{3,2,1,0:T(8,128)(2,1)S(1)} %divide_convert_fusion), channel_id=1, replica_groups=mesh['z'=8,'xh'=2,'y'=4,'xl'=2,'c'=2] {'z'}, dimensions={0} | all-to-all | bytes 1048576 | tf_op jit(solution)/shard_map/all_to_all | solution.py:193
  280.8 1.0 copy.26
  (6 shorter events, 0.1 us)
Async XLA Ops:
  6.5 207.3 %all-gather.3.cloned.1.call-start = ((), (), s32[]{:S(2)}) async-start(), calls=%async_computation.3 | async-start | bytes 8912896 | tf_op jit(solution)/shard_map/all_gather | solution.py:181
  36.7 19.4 %all-to-all-start = ((bf16[8,2,128,128]{3,2,1,0:T(8,128)(2,1)}), bf16[8,2,128,128]{3,2,1,0:T(8,128)(2,1)S(1)}, u32[]{:S(2)}, u32[]{:S(2)}) async-start(bf16[8,2,128,128]{3,2,1,0:T(8,128)(2,1)} %bitcast.4), calls=%async_computation | async-start | bytes 1048576 | tf_op jit(solution)/shard_map/all_to_all | solution.py:183
  56.1 1.9 collective-permute-start
  253.8 2.1 collective-permute-start.2
  253.9 2.0 collective-permute-start.1
Sparse Core Ops, SparseCore 0:
  34.7 179.0 all-gather.2
